TPU v7x, 512 devices: a whole 4x4x16 slice. The times are simulated.
512 devices in a mesh: dp: 256 (over y, x, z), ctx: 2 (over core).
Axes of the slice: x: 4, y: 4, z: 16, core: 2. Of those that a mesh axis runs over, the one named last changes fastest.
Arguments:
- q_weight: bfloat16 [256, 256, 2, 576], P(None, 'dp', 'ctx'), may hold values from -6 to 6
- kv_weight: bfloat16 [256, 256, 2, 256], P(None, 'dp', 'ctx'), may hold values from -6 to 6
- q_grad: bfloat16 [2, 256, 256, 2, 576], P('ctx', None, 'dp'), may hold values from -6 to 6
- kv_grad: bfloat16 [2, 256, 256, 2, 256], P('ctx', None, 'dp'), may hold values from -6 to 6
- q_moment: float32 [256, 2, 256, 576], P(None, 'ctx', 'dp')
- kv_moment: float32 [256, 2, 256, 256], P(None, 'ctx', 'dp')
- logit_part: float32 [256, 2, 256], P('dp', 'ctx'), may hold values from 5 to 300, as said below
- slot_table: int32 [256], replicated, may hold values from 0 to 255, each once
Outputs:
- q_weight_out: bfloat16 [256, 256, 2, 576], P(None, 'dp', 'ctx')
- kv_weight_out: bfloat16 [256, 256, 2, 256], P(None, 'dp', 'ctx')
- q_moment_out: float32 [256, 2, 256, 576], P(None, 'ctx', 'dp')
- kv_moment_out: float32 [256, 2, 256, 256], P(None, 'ctx', 'dp')
Inputs may be any that keep to these rules, and one draw needn't show every extreme that they name: `slot_table`: a permutation; the block in slot s is owned by index s // 1 of dp. `logit_part`: positive.
All inputs are finite; a program needn't handle non-finite values.
Results may differ from a plain program's by a relative error of at most 0.023.
Values may be sent and summed in bfloat16 or wider, within the bound.
A program may use at most 64 MiB of HBM per device.

v0:
```python
import math

import jax
import jax.numpy as jnp
from jax import lax
from jax.experimental import pallas as pl
from jax.experimental.pallas import tpu as pltpu
from jax.sharding import PartitionSpec as P

NOPE = 128
ITERS = 5
QDIM = 192
KVDIM = 256

GY = 4
GX = 4
GZ = 16
GYX = GY * GX
QRANK = 1536
KVRANK = 512

newton_a = 3.4445
newton_b = -4.775
newton_c = 2.0315
momentum_rate = 0.95
learn_rate = 2.0
weight_decay = 0.1
rms_match = 0.2
clip_limit = 100.0
norm_eps = 1e-06

MESH = pl.DeviceIdType.MESH
BF = jnp.bfloat16
F32 = jnp.float32

CHUNKS = (256, 384, 256)
Q_CUTS = ((0, 256), (256, 640))
Q_PAD = 640


def nt(a, b):
    return lax.dot_general(a, b, (((1,), (1,)), ((), ())), preferred_element_type=F32)


def nn(a, b):
    return lax.dot_general(a, b, (((1,), (0,)), ((), ())), preferred_element_type=F32)


def tn(a, b):
    return lax.dot_general(a, b, (((0,), (0,)), ((), ())), preferred_element_type=F32)


def one_hot(mask):
    return jnp.where(mask, 1.0, 0.0).astype(BF)


def kernel(
    slot_ref, logit_ref, gq_ref, gkv_ref, mq_ref, mkv_ref, wq_ref, wkv_ref,
    wq_out, wkv_out, mq_out, mkv_out,
    xq, xkv, qs, place, swap,
    fsa0, fsa1, fsa2, fra0, fra1, fra2, fsb0, fsb1, fsb2, frb0, frb1, frb2,
    bsa0, bsa1, bsa2, bra0, bra1, bra2, bsb0, bsb1, bsb2, brb0, brb1, brb2,
    mbq, mpq, mbkv, mpkv, xt, xk, xf,
    lz, lm, ly, lc, lp,
    core_send, core_recv, log_send, log_recv, fa_send, fa_recv, fb_send, fb_recv,
    ba_send, ba_recv, bb_send, bb_recv,
):
    fsa, fra, fsb, frb = (fsa0, fsa1, fsa2), (fra0, fra1, fra2), (fsb0, fsb1, fsb2), (frb0, frb1, frb2)
    bsa, bra, bsb, brb = (bsa0, bsa1, bsa2), (bra0, bra1, bra2), (bsb0, bsb1, bsb2), (brb0, brb1, brb2)
    me = lax.axis_index("dp")
    core = lax.axis_index("ctx")
    other = 1 - core
    z = lax.rem(me, GZ)
    yx = lax.div(me, GZ)
    y = lax.div(yx, GX)
    x = lax.rem(yx, GX)
    total = GZ * GYX
    heads = slot_ref.shape[1]
    qw = mq_ref.shape[0]

    def z_peer(i):
        step = i // 2 + 1
        sign = 1 - 2 * (i % 2)
        return lax.rem(z + sign * step + GZ, GZ)

    def yx_peer(i):
        j = i + 1
        return lax.rem(y + j // GX, GY) * GX + lax.rem(x + j % GX, GX)

    def z_dev(zt):
        return (yx * GZ + zt, core)

    def yx_dev(yxt):
        return (yxt * GZ + z, core)

    barrier = pltpu.get_barrier_semaphore()

    def greet_z(i, carry):
        pl.semaphore_signal(barrier, inc=1, device_id=z_dev(z_peer(i)), device_id_type=MESH)
        return carry

    def greet_yx(i, carry):
        pl.semaphore_signal(barrier, inc=1, device_id=yx_dev(yx_peer(i)), device_id_type=MESH)
        return carry

    pl.semaphore_signal(barrier, inc=1, device_id=(me, other), device_id_type=MESH)
    lax.fori_loop(0, GZ - 1, greet_z, 0)
    lax.fori_loop(0, GYX - 1, greet_yx, 0)

    rows = lax.broadcasted_iota(jnp.int32, (total, heads), 0)
    place[...] = one_hot(slot_ref[...] == (rows % GYX) * GZ + rows // GYX)
    rows = lax.broadcasted_iota(jnp.int32, (total, total), 0)
    cols = lax.broadcasted_iota(jnp.int32, (total, total), 1)
    swap[...] = one_hot(cols == (rows % GZ) * GYX + rows // GZ)
    qs[qw:, :] = jnp.zeros((Q_PAD - qw, heads), BF)
    xf[qw:, :] = jnp.zeros((Q_PAD - qw, total), BF)

    pl.semaphore_wait(barrier, GZ - 1 + GYX - 1 + 1)

    def to_core(src, dst, slot):
        return pltpu.make_async_remote_copy(
            src_ref=src, dst_ref=dst, send_sem=core_send.at[slot], recv_sem=core_recv.at[slot],
            device_id=(me, other), device_id_type=MESH,
        )

    core_q = to_core(gq_ref.at[other], xq, 0)
    core_kv = to_core(gkv_ref.at[other], xkv, 1)
    core_q.start()
    core_kv.start()

    def all_z(src, dst, send_sem, recv_sem):
        def body(i, carry):
            zt = z_peer(i)
            pltpu.make_async_remote_copy(
                src_ref=src.at[pl.ds(pl.multiple_of(zt * GYX, GYX), GYX)],
                dst_ref=dst.at[pl.ds(pl.multiple_of(z * GYX, GYX), GYX)],
                send_sem=send_sem, recv_sem=recv_sem,
                device_id=z_dev(zt), device_id_type=MESH,
            ).start()
            return carry

        lax.fori_loop(0, GZ - 1, body, 0)
        mine = pl.ds(pl.multiple_of(z * GYX, GYX), GYX)
        dst[mine, :] = src[mine, :]

    def all_yx(src, dst, send_sem, recv_sem):
        def body(i, carry):
            yxt = yx_peer(i)
            pltpu.make_async_remote_copy(
                src_ref=src.at[pl.ds(pl.multiple_of(yxt * GZ, GZ), GZ)],
                dst_ref=dst.at[pl.ds(pl.multiple_of(yx * GZ, GZ), GZ)],
                send_sem=send_sem, recv_sem=recv_sem,
                device_id=yx_dev(yxt), device_id_type=MESH,
            ).start()
            return carry

        lax.fori_loop(0, GYX - 1, body, 0)
        mine = pl.ds(pl.multiple_of(yx * GZ, GZ), GZ)
        dst[mine, :] = src[mine, :]

    def wait_rows(buf, count, sem):
        view = buf.at[pl.ds(0, count)]
        pltpu.make_async_copy(view, view, sem).wait()

    def wait_z(buf, sem):
        wait_rows(buf, (GZ - 1) * GYX, sem)

    def wait_yx(buf, sem):
        wait_rows(buf, (GYX - 1) * GZ, sem)

    def logits_z(i, carry):
        pltpu.make_async_remote_copy(
            src_ref=logit_ref, dst_ref=lz.at[z], send_sem=log_send.at[0], recv_sem=log_recv.at[0],
            device_id=z_dev(z_peer(i)), device_id_type=MESH,
        ).start()
        return carry

    def logits_yx(i, carry):
        pltpu.make_async_remote_copy(
            src_ref=lm, dst_ref=ly.at[yx], send_sem=log_send.at[1], recv_sem=log_recv.at[1],
            device_id=yx_dev(yx_peer(i)), device_id_type=MESH,
        ).start()
        return carry

    lax.fori_loop(0, GZ - 1, logits_z, 0)
    lz[z] = logit_ref[...]

    core_q.wait()
    qs[:qw, :] = (gq_ref[core].astype(F32) + xq[...].astype(F32)).astype(BF)
    for n, (low, high) in enumerate(Q_CUTS):
        fsa[n][...] = nt(place[...], qs[low:high, :]).astype(BF)
        all_z(fsa[n], fra[n], fa_send.at[n], fa_recv.at[n])
    core_kv.wait()
    kvs = (gkv_ref[core].astype(F32) + xkv[...].astype(F32)).astype(BF)
    fsa[2][...] = nn(place[...], kvs).astype(BF)
    all_z(fsa[2], fra[2], fa_send.at[2], fa_recv.at[2])

    pltpu.make_async_copy(
        lz.at[pl.ds(0, GZ - 1)], lz.at[pl.ds(0, GZ - 1)], log_recv.at[0]
    ).wait()
    lm[...] = jnp.max(lz[...], axis=0)
    lax.fori_loop(0, GYX - 1, logits_yx, 0)
    ly[yx] = lm[...]

    def forward_mid(n):
        wait_z(fra[n], fa_recv.at[n])
        fsb[n][...] = nn(swap[...], fra[n][...]).astype(BF)
        all_yx(fsb[n], frb[n], fb_send.at[n], fb_recv.at[n])

    forward_mid(0)
    forward_mid(1)

    squares = jnp.zeros((1, 1), F32)
    for n, (low, high) in enumerate(Q_CUTS):
        wait_yx(frb[n], fb_recv.at[n])
        real = min(high, qw) - low
        size = high - low
        eye = one_hot(
            lax.broadcasted_iota(jnp.int32, (real, size), 0) == lax.broadcasted_iota(jnp.int32, (real, size), 1)
        )
        fresh = momentum_rate * mq_ref[low : low + real, :] + nt(eye, frb[n][...])
        mq_out[low : low + real, :] = fresh
        mbq[low : low + real, :] = fresh.astype(BF)
        squares = squares + jnp.sum(fresh * fresh, keepdims=True)
    core_mq = to_core(mbq, mpq, 2)
    core_mq.start()
    core_mq.wait()
    theirs = mpq[...].astype(F32)
    squares = squares + jnp.sum(theirs * theirs, keepdims=True)
    scale = 1.0 / (jnp.sqrt(squares) + norm_eps)
    parts = qw // QDIM
    for j in range(parts):
        band = slice(j * QDIM, (j + 1) * QDIM)
        xt[:, j * total : (j + 1) * total] = (mq_out[band, :] * scale).astype(BF)
        lane = (parts + j) * total
        xt[:, lane : lane + total] = (mpq[band, :].astype(F32) * scale).astype(BF)

    def newton(ref, width):
        gram = nt(ref[...], ref[...]).astype(BF)
        mixer = (newton_b * gram.astype(F32) + newton_c * nn(gram, gram)).astype(BF)
        for low in range(0, width, total):
            piece = ref[:, low : low + total]
            yield low, (newton_a * piece.astype(F32) + nn(mixer, piece)).astype(BF)

    for iteration in range(ITERS - 1):
        for low, piece in newton(xt, 2 * parts * total):
            xt[:, low : low + total] = piece
    for low, piece in newton(xt, parts * total):
        j = low // total
        xf[j * QDIM : (j + 1) * QDIM, :] = piece

    for n, (low, high) in enumerate(Q_CUTS):
        bsa[n][...] = nt(swap[...], xf[low:high, :]).astype(BF)
        all_z(bsa[n], bra[n], ba_send.at[n], ba_recv.at[n])

    forward_mid(2)
    wait_yx(frb[2], fb_recv.at[2])
    fresh = momentum_rate * mkv_ref[...] + frb[2][...].astype(F32)
    mkv_out[...] = fresh
    mbkv[...] = fresh.astype(BF)
    core_mkv = to_core(mbkv, mpkv, 3)
    core_mkv.start()
    squares = jnp.sum(fresh * fresh, keepdims=True)
    core_mkv.wait()
    theirs = mpkv[...].astype(F32)
    squares = squares + jnp.sum(theirs * theirs, keepdims=True)
    scale = 1.0 / (jnp.sqrt(squares) + norm_eps)
    eye = one_hot(
        lax.broadcasted_iota(jnp.int32, (KVDIM, KVDIM), 0) == lax.broadcasted_iota(jnp.int32, (KVDIM, KVDIM), 1)
    )
    xk[:, :total] = nt(eye, (mkv_out[...] * scale).astype(BF)).astype(BF)
    xk[:, total:] = nt(eye, (theirs * scale).astype(BF)).astype(BF)
    for iteration in range(ITERS - 1):
        for low, piece in newton(xk, 2 * total):
            xk[:, low : low + total] = piece
    for low, piece in newton(xk, total):
        bsa[2][...] = nt(swap[...], piece).astype(BF)
    all_z(bsa[2], bra[2], ba_send.at[2], ba_recv.at[2])

    def back_mid(n):
        wait_z(bra[n], ba_recv.at[n])
        bsb[n][...] = nn(swap[...], bra[n][...]).astype(BF)
        all_yx(bsb[n], brb[n], bb_send.at[n], bb_recv.at[n])

    back_mid(0)
    back_mid(1)

    pltpu.make_async_copy(
        ly.at[pl.ds(0, GYX - 1)], ly.at[pl.ds(0, GYX - 1)], log_recv.at[1]
    ).wait()
    lc[...] = jnp.max(ly[...], axis=0)
    core_peak = to_core(lc, lp, 4)
    core_peak.start()
    core_peak.wait()
    peak = jnp.maximum(lc[...], lp[...])
    clip = jnp.minimum(1.0, clip_limit / peak)
    root = jnp.sqrt(clip)

    back_mid(2)

    pick = one_hot(slot_ref[...] == lax.broadcasted_iota(jnp.int32, (total, heads), 0))
    scale = rms_match * math.sqrt(max(QRANK, QDIM))
    for n, (low, high) in enumerate(Q_CUTS):
        wait_yx(brb[n], bb_recv.at[n])
        real = min(high, qw) - low
        size = high - low
        update = tn(brb[n][...], pick)[:real, :]
        wide = wq_ref[low : low + real, :].astype(F32)
        fresh = wide - learn_rate * (scale * update + weight_decay * wide)
        column = (lax.broadcasted_iota(jnp.int32, (real, heads), 0) + low) % QDIM
        factor = jnp.where(column < NOPE, root, clip)
        wq_out[low : low + real, :] = (fresh * factor).astype(BF)

    scale = rms_match * math.sqrt(max(KVRANK, KVDIM))
    wait_yx(brb[2], bb_recv.at[2])
    update = tn(pick, brb[2][...])
    wide = wkv_ref[...].astype(F32)
    fresh = wide - learn_rate * (scale * update + weight_decay * wide)
    root_rows = jnp.transpose(jnp.broadcast_to(root, (NOPE, heads)))
    wkv_out[:, :NOPE] = (fresh[:, :NOPE] * root_rows).astype(BF)
    wkv_out[:, NOPE:] = fresh[:, NOPE:].astype(BF)

    for n in range(3):
        wait_z(fsa[n], fa_send.at[n])
        wait_z(bsa[n], ba_send.at[n])
        wait_yx(fsb[n], fb_send.at[n])
        wait_yx(bsb[n], bb_send.at[n])
    pltpu.make_async_copy(
        lz.at[pl.ds(0, GZ - 1)], lz.at[pl.ds(0, GZ - 1)], log_send.at[0]
    ).wait()
    pltpu.make_async_copy(
        ly.at[pl.ds(0, GYX - 1)], ly.at[pl.ds(0, GYX - 1)], log_send.at[1]
    ).wait()


def local(q_weight, kv_weight, q_grad, kv_grad, q_moment, kv_moment, logit_part, slot_table):
    heads = q_weight.shape[0]
    total = q_moment.shape[0]
    qw = q_weight.shape[3]
    kvw = kv_weight.shape[3]
    args = (
        slot_table.reshape(1, heads),
        logit_part.reshape(1, heads),
        jnp.transpose(q_grad.reshape(heads, 2, qw), (1, 2, 0)),
        jnp.transpose(kv_grad.reshape(heads, 2, kvw), (1, 0, 2)),
        jnp.transpose(q_moment.reshape(total, qw)),
        kv_moment.reshape(total, kvw),
        jnp.transpose(q_weight.reshape(heads, qw)),
        kv_weight.reshape(heads, kvw),
    )
    out_shape = (
        jax.ShapeDtypeStruct((qw, heads), BF),
        jax.ShapeDtypeStruct((heads, kvw), BF),
        jax.ShapeDtypeStruct((qw, total), F32),
        jax.ShapeDtypeStruct((total, kvw), F32),
    )
    travel = [pltpu.VMEM((total, width), BF) for _ in range(8) for width in CHUNKS]
    parts = qw // QDIM
    vmem = pl.BlockSpec(memory_space=pltpu.VMEM)
    wq, wkv, mq, mkv = pl.pallas_call(
        kernel,
        out_shape=out_shape,
        in_specs=[vmem] * len(args),
        out_specs=tuple([vmem] * 4),
        scratch_shapes=[
            pltpu.VMEM((qw, heads), BF),
            pltpu.VMEM((heads, kvw), BF),
            pltpu.VMEM((Q_PAD, heads), BF),
            pltpu.VMEM((total, heads), BF),
            pltpu.VMEM((total, total), BF),
            *travel,
            pltpu.VMEM((qw, total), BF),
            pltpu.VMEM((qw, total), BF),
            pltpu.VMEM((total, kvw), BF),
            pltpu.VMEM((total, kvw), BF),
            pltpu.VMEM((QDIM, 2 * parts * total), BF),
            pltpu.VMEM((KVDIM, 2 * total), BF),
            pltpu.VMEM((Q_PAD, total), BF),
            pltpu.VMEM((GZ, 1, heads), F32),
            pltpu.VMEM((1, heads), F32),
            pltpu.VMEM((GYX, 1, heads), F32),
            pltpu.VMEM((1, heads), F32),
            pltpu.VMEM((1, heads), F32),
            pltpu.SemaphoreType.DMA((5,)),
            pltpu.SemaphoreType.DMA((5,)),
            pltpu.SemaphoreType.DMA((2,)),
            pltpu.SemaphoreType.DMA((2,)),
            *[pltpu.SemaphoreType.DMA((3,)) for _ in range(8)],
        ],
        compiler_params=pltpu.CompilerParams(
            collective_id=0, has_side_effects=True, vmem_limit_bytes=48 * 1024 * 1024
        ),
        cost_estimate=pl.CostEstimate(flops=4_000_000_000, bytes_accessed=4_000_000, transcendentals=0),
    )(*args)
    return (
        jnp.transpose(wq).reshape(q_weight.shape),
        wkv.reshape(kv_weight.shape),
        jnp.transpose(mq).reshape(q_moment.shape),
        mkv.reshape(kv_moment.shape),
    )


def solution(mesh):
    in_specs = (
        P(None, "dp", "ctx", None),
        P(None, "dp", "ctx", None),
        P("ctx", None, "dp", None, None),
        P("ctx", None, "dp", None, None),
        P(None, "ctx", "dp", None),
        P(None, "ctx", "dp", None),
        P("dp", "ctx", None),
        P(),
    )
    out_specs = (
        P(None, "dp", "ctx", None),
        P(None, "dp", "ctx", None),
        P(None, "ctx", "dp", None),
        P(None, "ctx", "dp", None),
    )
    return jax.shard_map(local, mesh=mesh, in_specs=in_specs, out_specs=out_specs, check_vma=False)
```

profile of v0, /device:TPU:1, one launch (start us, length us, event | category | flops | bytes accessed | tf_op | source)
XLA Modules:
  0.0 88.8 jit_solution(3500766505101782700)
XLA Ops:
  0.6 0.0 copy-start
  0.6 1.0 %copy.18 = bf16[1,256,1,2,256]{4,1,3,2,0:T(8,128)(2,1)S(1)} copy(bf16[1,256,1,2,256]{4,3,2,1,0:T(2,128)(2,1)} %param.11) | data formatting | bytes 524288 | tf_op args[3]
  1.7 0.0 copy-start.2
  1.7 0.0 copy-start.3
  1.7 0.0 copy-start.5
  1.7 1.0 %copy.17 = f32[256,1,1,256]{3,0,1,2:T(8,128)S(1)} copy(f32[256,1,1,256]{3,2,1,0:T(1,128)} %param.13) | data formatting | bytes 524288
  2.7 0.0 copy-start.4
  2.8 0.0 copy-done
  2.8 0.0 copy-done.2
  2.8 0.0 copy-done.3
  2.8 0.0 copy-done.5
  2.8 0.6 copy-done.4
  3.4 0.0 copy-start.1
  3.4 1.1 %copy-done.1 = f32[256,1,1,576]{0,3,2,1:T(8,128)S(1)} copy-done((f32[256,1,1,576]{0,3,2,1:T(8,128)S(1)}, f32[256,1,1,576]{0,3,2,1:T(8,128)}, u32[]{:S(2)}) %copy-start.1) | copy-done | bytes 589848
  4.5 81.1 %shard_map.111 = (bf16[576,256]{1,0:T(8,128)(2,1)S(1)}, bf16[256,256]{1,0:T(8,128)(2,1)S(1)}, f32[576,256]{1,0:T(8,128)S(1)}, f32[256,256]{1,0:T(8,128)S(1)}) custom-call(s32[1,256]{1,0:T(1,128)S(1)} %bitcast.38, f32[1,256]{1,0:T(1,128)S(1)} %bitcast.39, bf16[2,576,256]{2,1,0:T(8,128)(2,1)S(1)} %bitcast.34, bf16[2,256,256]{2,1,0:T(8,128)(2,1)S(1)} %bitcast.31, ...), custom_call_target="tpu_custom_call" | custom-call | flops 4000000000 | bytes 4000000 | tf_op jit(solution)/shard_map/pallas_call | solution.py:360
  85.6 1.0 %copy.13 = f32[256,1,1,256]{3,2,1,0:T(1,128)} copy(f32[256,1,1,256]{3,0,2,1:T(8,128)S(1)} %bitcast.30) | data formatting | bytes 524288
  86.6 0.7 copy.22
  87.3 0.7 copy.23
  88.0 0.8 copy.24
Async XLA Ops:
  0.6 2.1 %copy-start = (bf16[1,256,1,2,576]{1,4,3,2,0:T(8,128)(2,1)S(1)}, bf16[1,256,1,2,576]{1,4,3,2,0:T(8,128)(2,1)}, u32[]{:S(2)}) copy-start(bf16[1,256,1,2,576]{1,4,3,2,0:T(8,128)(2,1)} %param.10) | copy-start | bytes 1769476
  1.7 1.1 %copy-start.2 = (bf16[256,1,1,576]{0,3,2,1:T(8,128)(2,1)S(1)}, bf16[256,1,1,576]{0,3,2,1:T(8,128)(2,1)}, u32[]{:S(2)}) copy-start(bf16[256,1,1,576]{0,3,2,1:T(8,128)(2,1)} %param.8) | copy-start | bytes 884740
  1.7 1.1 %copy-start.3 = (bf16[256,1,1,256]{3,0,2,1:T(8,128)(2,1)S(1)}, bf16[256,1,1,256]{3,0,2,1:T(8,128)(2,1)}, u32[]{:S(2)}) copy-start(bf16[256,1,1,256]{3,0,2,1:T(8,128)(2,1)} %param.9) | copy-start | bytes 393220
  1.7 1.1 %copy-start.5 = (f32[1,1,256]{2,1,0:T(1,128)S(1)}, f32[1,1,256]{2,1,0:T(1,128)}, u32[]{:S(2)}) copy-start(f32[1,1,256]{2,1,0:T(1,128)} %param.14) | copy-start | bytes 3076
  2.7 0.7 copy-start.4
  3.4 1.1 %copy-start.1 = (f32[256,1,1,576]{0,3,2,1:T(8,128)S(1)}, f32[256,1,1,576]{0,3,2,1:T(8,128)}, u32[]{:S(2)}) copy-start(f32[256,1,1,576]{0,3,2,1:T(8,128)} %param.12) | copy-start | bytes 1769476
where the time goes:
time: 89.3 us; the launch traced here: 88.8 us
  Pallas kernels  81.1 us (91%)
  local copies, waits for them, and re-layouts  6.94 us (8%)
    pallas_call x1, Pallas kernels, local(): pl.pallas_call(kernel, out_shape=out_shape, in_specs=[vmem] * len(args),...  81.1 us
    unnamed x18, local copies, waits for them, and re-layouts  6.94 us

commit v1 on v0

v1 whole, which is shorter than its diff:
```python
import math

import jax
import jax.numpy as jnp
from jax import lax
from jax.experimental import pallas as pl
from jax.experimental.pallas import tpu as pltpu
from jax.sharding import PartitionSpec as P

NOPE = 128
ITERS = 5
QDIM = 192
KVDIM = 256

GY = 4
GX = 4
GZ = 16
GYX = GY * GX
QRANK = 1536
KVRANK = 512

newton_a = 3.4445
newton_b = -4.775
newton_c = 2.0315
momentum_rate = 0.95
learn_rate = 2.0
weight_decay = 0.1
rms_match = 0.2
clip_limit = 100.0
norm_eps = 1e-06

MESH = pl.DeviceIdType.MESH
BF = jnp.bfloat16
F32 = jnp.float32

CHUNKS = (256, 384, 256)
Q_CUTS = ((0, 256), (256, 640))
Q_PAD = 640
VMEM_LIMIT = 62 * 1024 * 1024


def nt(a, b):
    return lax.dot_general(a, b, (((1,), (1,)), ((), ())), preferred_element_type=F32)


def nn(a, b):
    return lax.dot_general(a, b, (((1,), (0,)), ((), ())), preferred_element_type=F32)


def tn(a, b):
    return lax.dot_general(a, b, (((0,), (0,)), ((), ())), preferred_element_type=F32)


def one_hot(mask):
    return jnp.where(mask, 1.0, 0.0).astype(BF)


def kernel(
    slot_hbm, logit_hbm, gq_hbm, gkv_hbm, mq_hbm, mkv_hbm,
    uq_hbm, ukv_hbm, mq_new_hbm, mkv_new_hbm, peak_hbm,
    slot_ref, logit_ref, gq_ref, gkv_ref, mq_ref, mkv_ref,
    uq_out, ukv_out, mq_out, mkv_out, peak_out,
    xq, xkv, okv, skv, qs, place, swap,
    fsa0, fsa1, fsa2, fra0, fra1, fra2, fsb0, fsb1, fsb2, frb0, frb1, frb2,
    bsa0, bsa1, bsa2, bra0, bra1, bra2, bsb0, bsb1, bsb2, brb0, brb1, brb2,
    mbq, mpq, mbkv, mpkv, xt, xk, xf,
    lz, lm, ly, lc, lp,
    load_sem, store_sem, core_send, core_recv, log_send, log_recv, fa_send, fa_recv, fb_send, fb_recv,
    ba_send, ba_recv, bb_send, bb_recv,
):
    fsa, fra, fsb, frb = (fsa0, fsa1, fsa2), (fra0, fra1, fra2), (fsb0, fsb1, fsb2), (frb0, frb1, frb2)
    bsa, bra, bsb, brb = (bsa0, bsa1, bsa2), (bra0, bra1, bra2), (bsb0, bsb1, bsb2), (brb0, brb1, brb2)
    me = lax.axis_index("dp")
    core = lax.axis_index("ctx")
    other = 1 - core
    z = lax.rem(me, GZ)
    yx = lax.div(me, GZ)
    y = lax.div(yx, GX)
    x = lax.rem(yx, GX)
    total = GZ * GYX
    heads = slot_ref.shape[1]
    qw = mq_ref.shape[0]
    lanes = mkv_ref.shape[1]
    halves = KVDIM // lanes

    def z_peer(i):
        j = i + 1
        step = GZ // 2 - j // 2
        sign = 1 - 2 * (j % 2)
        return lax.rem(z + sign * step + GZ, GZ)

    def yx_peer(i):
        j = GYX - 1 - i
        return lax.rem(y + j // GX, GY) * GX + lax.rem(x + j % GX, GX)

    def z_dev(zt):
        return (yx * GZ + zt, core)

    def yx_dev(yxt):
        return (yxt * GZ + z, core)

    barrier = pltpu.get_barrier_semaphore()

    def greet_z(i, carry):
        pl.semaphore_signal(barrier, inc=1, device_id=z_dev(z_peer(i)), device_id_type=MESH)
        return carry

    def greet_yx(i, carry):
        pl.semaphore_signal(barrier, inc=1, device_id=yx_dev(yx_peer(i)), device_id_type=MESH)
        return carry

    lax.fori_loop(0, GZ - 1, greet_z, 0)
    lax.fori_loop(0, GYX - 1, greet_yx, 0)
    pl.semaphore_signal(barrier, inc=1, device_id=(me, other), device_id_type=MESH)

    loads = [
        pltpu.make_async_copy(src, dst, load_sem.at[n])
        for n, (src, dst) in enumerate(
            (
                (gq_hbm, gq_ref), (gkv_hbm, gkv_ref), (mq_hbm, mq_ref), (mkv_hbm, mkv_ref),
                (slot_hbm, slot_ref), (logit_hbm, logit_ref),
            )
        )
    ]
    stores = [
        pltpu.make_async_copy(src, dst, store_sem.at[n])
        for n, (src, dst) in enumerate(
            (
                (uq_out, uq_hbm), (ukv_out, ukv_hbm), (mq_out, mq_new_hbm), (mkv_out, mkv_new_hbm),
                (peak_out, peak_hbm),
            )
        )
    ]
    for n in (4, 1, 0, 5, 2, 3):
        loads[n].start()

    loads[4].wait()
    rows = lax.broadcasted_iota(jnp.int32, (total, heads), 0)
    place[...] = one_hot(slot_ref[...] == (rows % GYX) * GZ + rows // GYX)
    rows = lax.broadcasted_iota(jnp.int32, (total, total), 0)
    cols = lax.broadcasted_iota(jnp.int32, (total, total), 1)
    swap[...] = one_hot(cols == (rows % GZ) * GYX + rows // GZ)
    qs[qw:, :] = jnp.zeros((Q_PAD - qw, heads), BF)
    xf[qw:, :] = jnp.zeros((Q_PAD - qw, total), BF)

    loads[1].wait()
    cols = lax.broadcasted_iota(jnp.int32, (heads, 2 * halves * heads), 1)
    rows = lax.broadcasted_iota(jnp.int32, (heads, 2 * halves * heads), 0)
    offset = cols - 2 * halves * rows
    for t in range(halves):
        band = slice(t * lanes, (t + 1) * lanes)
        okv[:, band] = nn(one_hot(offset == 2 * t + other), gkv_ref[...]).astype(BF)
        skv[:, band] = nn(one_hot(offset == 2 * t + core), gkv_ref[...]).astype(BF)
    loads[0].wait()
    loads[5].wait()

    pl.semaphore_wait(barrier, GZ - 1 + GYX - 1 + 1)

    def to_core(src, dst, slot):
        return pltpu.make_async_remote_copy(
            src_ref=src, dst_ref=dst, send_sem=core_send.at[slot], recv_sem=core_recv.at[slot],
            device_id=(me, other), device_id_type=MESH,
        )

    spans = tuple(slice(low, min(high, qw)) for low, high in Q_CUTS)
    core_q = [to_core(gq_ref.at[other, span], xq.at[span], n) for n, span in enumerate(spans)]
    core_kv = to_core(okv, xkv, 2)
    for copy in core_q:
        copy.start()
    core_kv.start()

    def send_z(src, dst, send_sem, recv_sem, zt):
        pltpu.make_async_remote_copy(
            src_ref=src.at[pl.ds(pl.multiple_of(zt * GYX, GYX), GYX)],
            dst_ref=dst.at[pl.ds(pl.multiple_of(z * GYX, GYX), GYX)],
            send_sem=send_sem, recv_sem=recv_sem,
            device_id=z_dev(zt), device_id_type=MESH,
        ).start()

    def keep_z(src, dst):
        mine = pl.ds(pl.multiple_of(z * GYX, GYX), GYX)
        dst[mine, :] = src[mine, :]

    def some_z(n, parity):
        odd = lax.rem(z + parity, 2)

        def body(i, carry):
            j = i + 1 - odd
            step = GZ // 2 - odd - 2 * (j // 2)
            sign = 1 - 2 * (j % 2)
            send_z(fsa[n], fra[n], fa_send.at[n], fa_recv.at[n], lax.rem(z + sign * step + GZ, GZ))
            return carry

        lax.fori_loop(0, GZ // 2 - 1 + odd, body, 0)

    def all_z(src, dst, send_sem, recv_sem):
        def body(i, carry):
            send_z(src, dst, send_sem, recv_sem, z_peer(i))
            return carry

        lax.fori_loop(0, GZ - 1, body, 0)
        keep_z(src, dst)

    def all_yx(src, dst, send_sem, recv_sem):
        def body(i, carry):
            yxt = yx_peer(i)
            pltpu.make_async_remote_copy(
                src_ref=src.at[pl.ds(pl.multiple_of(yxt * GZ, GZ), GZ)],
                dst_ref=dst.at[pl.ds(pl.multiple_of(yx * GZ, GZ), GZ)],
                send_sem=send_sem, recv_sem=recv_sem,
                device_id=yx_dev(yxt), device_id_type=MESH,
            ).start()
            return carry

        lax.fori_loop(0, GYX - 1, body, 0)
        mine = pl.ds(pl.multiple_of(yx * GZ, GZ), GZ)
        dst[mine, :] = src[mine, :]

    def wait_rows(buf, count, sem):
        view = buf.at[pl.ds(0, count)]
        pltpu.make_async_copy(view, view, sem).wait()

    def wait_z(buf, sem):
        wait_rows(buf, (GZ - 1) * GYX, sem)

    def wait_yx(buf, sem):
        wait_rows(buf, (GYX - 1) * GZ, sem)

    def logits_z(i, carry):
        pltpu.make_async_remote_copy(
            src_ref=logit_ref, dst_ref=lz.at[z], send_sem=log_send.at[0], recv_sem=log_recv.at[0],
            device_id=z_dev(z_peer(i)), device_id_type=MESH,
        ).start()
        return carry

    def logits_yx(i, carry):
        pltpu.make_async_remote_copy(
            src_ref=lm, dst_ref=ly.at[yx], send_sem=log_send.at[1], recv_sem=log_recv.at[1],
            device_id=yx_dev(yx_peer(i)), device_id_type=MESH,
        ).start()
        return carry

    lax.fori_loop(0, GZ - 1, logits_z, 0)
    lz[z] = logit_ref[...]

    for n, (low, high) in enumerate(Q_CUTS):
        core_q[n].wait()
        span = spans[n]
        qs[span, :] = (gq_ref[core, span].astype(F32) + xq[span, :].astype(F32)).astype(BF)
        fsa[n][...] = nt(place[...], qs[low:high, :]).astype(BF)
        some_z(n, 0)
    for n in range(2):
        some_z(n, 1)
        keep_z(fsa[n], fra[n])
    core_kv.wait()
    kvs = (skv[...].astype(F32) + xkv[...].astype(F32)).astype(BF)
    fsa[2][...] = nn(place[...], kvs).astype(BF)
    some_z(2, 0)
    some_z(2, 1)
    keep_z(fsa[2], fra[2])

    def forward_mid(n):
        wait_z(fra[n], fa_recv.at[n])
        fsb[n][...] = nn(swap[...], fra[n][...]).astype(BF)
        all_yx(fsb[n], frb[n], fb_send.at[n], fb_recv.at[n])

    loads[2].wait()
    loads[3].wait()
    forward_mid(0)
    forward_mid(1)
    forward_mid(2)

    view = lz.at[pl.ds(0, GZ - 1)]
    pltpu.make_async_copy(view, view, log_recv.at[0]).wait()
    lm[...] = jnp.max(lz[...], axis=0)
    lax.fori_loop(0, GYX - 1, logits_yx, 0)
    ly[yx] = lm[...]

    squares = jnp.zeros((1, 1), F32)
    core_mq = [to_core(mbq.at[span], mpq.at[span], 3 + n) for n, span in enumerate(spans)]
    for n, (low, high) in enumerate(Q_CUTS):
        wait_yx(frb[n], fb_recv.at[n])
        span = spans[n]
        real = min(high, qw) - low
        size = high - low
        eye = one_hot(
            lax.broadcasted_iota(jnp.int32, (real, size), 0) == lax.broadcasted_iota(jnp.int32, (real, size), 1)
        )
        fresh = momentum_rate * mq_ref[span, :] + nt(eye, frb[n][...])
        mq_out[span, :] = fresh
        mbq[span, :] = fresh.astype(BF)
        core_mq[n].start()
        squares = squares + jnp.sum(fresh * fresh, keepdims=True)
    for n, span in enumerate(spans):
        core_mq[n].wait()
        theirs = mpq[span, :].astype(F32)
        squares = squares + jnp.sum(theirs * theirs, keepdims=True)
    stores[2].start()
    scale = 1.0 / (jnp.sqrt(squares) + norm_eps)
    parts = qw // QDIM
    for j in range(parts):
        band = slice(j * QDIM, (j + 1) * QDIM)
        xt[:, j * total : (j + 1) * total] = (mq_out[band, :] * scale).astype(BF)
        lane = (parts + j) * total
        xt[:, lane : lane + total] = (mpq[band, :].astype(F32) * scale).astype(BF)

    def newton(ref, width):
        gram = nt(ref[...], ref[...]).astype(BF)
        mixer = (newton_b * gram.astype(F32) + newton_c * nn(gram, gram)).astype(BF)
        for low in range(0, width, total):
            piece = ref[:, low : low + total]
            yield low, (newton_a * piece.astype(F32) + nn(mixer, piece)).astype(BF)

    for iteration in range(ITERS - 1):
        for low, piece in newton(xt, 2 * parts * total):
            xt[:, low : low + total] = piece
    for low, piece in newton(xt, parts * total):
        j = low // total
        xf[j * QDIM : (j + 1) * QDIM, :] = piece

    for n, (low, high) in enumerate(Q_CUTS):
        bsa[n][...] = nt(swap[...], xf[low:high, :]).astype(BF)
        all_z(bsa[n], bra[n], ba_send.at[n], ba_recv.at[n])

    wait_yx(frb[2], fb_recv.at[2])
    for t in range(halves):
        band = slice(t * lanes, (t + 1) * lanes)
        picked = pl.ds(t, total, stride=halves)
        fresh = momentum_rate * mkv_ref[picked, :] + frb[2][:, band].astype(F32)
        mkv_out[picked, :] = fresh
        mbkv[:, band] = fresh.astype(BF)
    core_mkv = to_core(mbkv, mpkv, 5)
    core_mkv.start()
    stores[3].start()
    ours = mkv_out[...]
    squares = jnp.sum(ours * ours, keepdims=True)
    eye = one_hot(
        lax.broadcasted_iota(jnp.int32, (lanes, lanes), 0) == lax.broadcasted_iota(jnp.int32, (lanes, lanes), 1)
    )
    core_mkv.wait()
    theirs = mpkv[...].astype(F32)
    squares = squares + jnp.sum(theirs * theirs, keepdims=True)
    scale = 1.0 / (jnp.sqrt(squares) + norm_eps)
    for t in range(halves):
        band = slice(t * lanes, (t + 1) * lanes)
        ours = mkv_out[pl.ds(t, total, stride=halves), :]
        xk[band, :total] = nt(eye, (ours * scale).astype(BF)).astype(BF)
        xk[band, total:] = nt(eye, (theirs[:, band] * scale).astype(BF)).astype(BF)
    for iteration in range(ITERS - 1):
        for low, piece in newton(xk, 2 * total):
            xk[:, low : low + total] = piece
    for low, piece in newton(xk, total):
        bsa[2][...] = nt(swap[...], piece).astype(BF)
    all_z(bsa[2], bra[2], ba_send.at[2], ba_recv.at[2])

    view = ly.at[pl.ds(0, GYX - 1)]
    pltpu.make_async_copy(view, view, log_recv.at[1]).wait()
    lc[...] = jnp.max(ly[...], axis=0)
    core_peak = to_core(lc, lp, 6)
    core_peak.start()
    core_peak.wait()
    peak_out[...] = jnp.maximum(lc[...], lp[...])
    stores[4].start()

    def back_mid(n):
        wait_z(bra[n], ba_recv.at[n])
        bsb[n][...] = nn(swap[...], bra[n][...]).astype(BF)
        all_yx(bsb[n], brb[n], bb_send.at[n], bb_recv.at[n])

    back_mid(0)
    back_mid(1)
    back_mid(2)

    pick = one_hot(slot_ref[...] == lax.broadcasted_iota(jnp.int32, (total, heads), 0))
    for n, (low, high) in enumerate(Q_CUTS):
        wait_yx(brb[n], bb_recv.at[n])
        real = min(high, qw) - low
        uq_out[spans[n], :] = tn(brb[n][...], pick)[:real, :].astype(BF)
    stores[0].start()
    for n in range(3):
        wait_z(fsa[n], fa_send.at[n])
        wait_z(bsa[n], ba_send.at[n])
        wait_yx(fsb[n], fb_send.at[n])
    view = lz.at[pl.ds(0, GZ - 1)]
    pltpu.make_async_copy(view, view, log_send.at[0]).wait()
    view = ly.at[pl.ds(0, GYX - 1)]
    pltpu.make_async_copy(view, view, log_send.at[1]).wait()
    wait_yx(brb[2], bb_recv.at[2])
    ukv_out[...] = tn(pick, brb[2][...]).astype(BF)
    stores[1].start()
    for n in range(3):
        wait_yx(bsb[n], bb_send.at[n])
    for store in stores:
        store.wait()


def finish(
    peak_hbm, uq_hbm, ukv_hbm, wq_hbm, wkv_hbm, mq_hbm, mkv_hbm,
    wq_out, wkv_out, mq_out, mkv_out,
    mq_ref, mkv_ref, peak_ref, uq_ref, ukv_ref, wq_ref, wkv_ref, new_q, new_kv, load_sem, sem,
):
    loads = [
        pltpu.make_async_copy(src, dst, load_sem.at[n])
        for n, (src, dst) in enumerate(
            (
                (peak_hbm, peak_ref), (uq_hbm, uq_ref), (wq_hbm, wq_ref), (ukv_hbm, ukv_ref), (wkv_hbm, wkv_ref),
                (mq_hbm, mq_ref), (mkv_hbm, mkv_ref),
            )
        )
    ]
    for load in loads:
        load.start()
    copies = [
        pltpu.make_async_copy(src, dst, sem.at[n])
        for n, (src, dst) in enumerate(
            ((mq_ref, mq_out), (mkv_ref, mkv_out), (new_q, wq_out), (new_kv, wkv_out))
        )
    ]
    qw, heads = wq_ref.shape
    for load in loads[:3]:
        load.wait()
    clip = jnp.minimum(1.0, clip_limit / peak_ref[...])
    root = jnp.sqrt(clip)
    scale = rms_match * math.sqrt(max(QRANK, QDIM))
    for low in range(0, qw, QDIM):
        for start, stop, factor in ((low, low + NOPE, root), (low + NOPE, low + QDIM, clip)):
            wide = wq_ref[start:stop, :].astype(F32)
            fresh = wide - learn_rate * (scale * uq_ref[start:stop, :].astype(F32) + weight_decay * wide)
            new_q[start:stop, :] = (fresh * factor).astype(BF)
    copies[2].start()
    for load in loads[5:]:
        load.wait()
    copies[0].start()
    copies[1].start()
    for load in loads[3:5]:
        load.wait()
    scale = rms_match * math.sqrt(max(KVRANK, KVDIM))
    wide = wkv_ref[...].astype(F32)
    fresh = wide - learn_rate * (scale * ukv_ref[...].astype(F32) + weight_decay * wide)
    root_rows = jnp.transpose(jnp.broadcast_to(root, (NOPE, heads)))
    new_kv[:, :NOPE] = (fresh[:, :NOPE] * root_rows).astype(BF)
    new_kv[:, NOPE:] = fresh[:, NOPE:].astype(BF)
    copies[3].start()
    for copy in copies:
        copy.wait()


def local(q_weight, kv_weight, q_grad, kv_grad, q_moment, kv_moment, logit_part, slot_table):
    heads = q_weight.shape[0]
    total = q_moment.shape[0]
    qw = q_weight.shape[3]
    kvw = kv_weight.shape[3]
    lanes = 128
    halves = kvw // lanes
    parts = qw // QDIM
    hbm = pl.BlockSpec(memory_space=pl.ANY)
    split = kv_grad.reshape(heads, 2, halves, lanes)
    travel = [pltpu.VMEM((total, width), BF) for _ in range(8) for width in CHUNKS]
    uq, ukv, mq, mkv, peak = pl.pallas_call(
        kernel,
        out_shape=(
            jax.ShapeDtypeStruct((qw, heads), BF),
            jax.ShapeDtypeStruct((heads, kvw), BF),
            jax.ShapeDtypeStruct((qw, total), F32),
            jax.ShapeDtypeStruct((halves * total, lanes), F32),
            jax.ShapeDtypeStruct((1, heads), F32),
        ),
        in_specs=[hbm] * 6,
        out_specs=tuple([hbm] * 5),
        scratch_shapes=[
            pltpu.VMEM((1, heads), jnp.int32),
            pltpu.VMEM((1, heads), F32),
            pltpu.VMEM((2, qw, heads), BF),
            pltpu.VMEM((2 * halves * heads, lanes), BF),
            pltpu.VMEM((qw, total), F32),
            pltpu.VMEM((halves * total, lanes), F32),
            pltpu.VMEM((qw, heads), BF),
            pltpu.VMEM((heads, kvw), BF),
            pltpu.VMEM((qw, total), F32),
            pltpu.VMEM((halves * total, lanes), F32),
            pltpu.VMEM((1, heads), F32),
            pltpu.VMEM((qw, heads), BF),
            pltpu.VMEM((heads, kvw), BF),
            pltpu.VMEM((heads, kvw), BF),
            pltpu.VMEM((heads, kvw), BF),
            pltpu.VMEM((Q_PAD, heads), BF),
            pltpu.VMEM((total, heads), BF),
            pltpu.VMEM((total, total), BF),
            *travel,
            pltpu.VMEM((qw, total), BF),
            pltpu.VMEM((qw, total), BF),
            pltpu.VMEM((total, kvw), BF),
            pltpu.VMEM((total, kvw), BF),
            pltpu.VMEM((QDIM, 2 * parts * total), BF),
            pltpu.VMEM((KVDIM, 2 * total), BF),
            pltpu.VMEM((Q_PAD, total), BF),
            pltpu.VMEM((GZ, 1, heads), F32),
            pltpu.VMEM((1, heads), F32),
            pltpu.VMEM((GYX, 1, heads), F32),
            pltpu.VMEM((1, heads), F32),
            pltpu.VMEM((1, heads), F32),
            pltpu.SemaphoreType.DMA((6,)),
            pltpu.SemaphoreType.DMA((5,)),
            pltpu.SemaphoreType.DMA((7,)),
            pltpu.SemaphoreType.DMA((7,)),
            pltpu.SemaphoreType.DMA((2,)),
            pltpu.SemaphoreType.DMA((2,)),
            *[pltpu.SemaphoreType.DMA((3,)) for _ in range(8)],
        ],
        compiler_params=pltpu.CompilerParams(
            collective_id=0, has_side_effects=True, vmem_limit_bytes=VMEM_LIMIT
        ),
        cost_estimate=pl.CostEstimate(flops=4_000_000_000, bytes_accessed=4_000_000, transcendentals=0),
    )(
        slot_table.reshape(1, heads),
        logit_part.reshape(1, heads),
        jnp.transpose(q_grad.reshape(heads, 2, qw), (1, 2, 0)),
        jnp.transpose(split, (0, 2, 1, 3)).reshape(2 * halves * heads, lanes),
        jnp.transpose(q_moment.reshape(total, qw)),
        kv_moment.reshape(halves * total, lanes),
    )
    wq, wkv, mq, mkv = pl.pallas_call(
        finish,
        out_shape=(
            jax.ShapeDtypeStruct((qw, heads), BF),
            jax.ShapeDtypeStruct((heads, kvw), BF),
            jax.ShapeDtypeStruct((qw, total), F32),
            jax.ShapeDtypeStruct((halves * total, lanes), F32),
        ),
        in_specs=[hbm] * 7,
        out_specs=tuple([hbm] * 4),
        scratch_shapes=[
            pltpu.VMEM((qw, total), F32),
            pltpu.VMEM((halves * total, lanes), F32),
            pltpu.VMEM((1, heads), F32),
            pltpu.VMEM((qw, heads), BF),
            pltpu.VMEM((heads, kvw), BF),
            pltpu.VMEM((qw, heads), BF),
            pltpu.VMEM((heads, kvw), BF),
            pltpu.VMEM((qw, heads), BF),
            pltpu.VMEM((heads, kvw), BF),
            pltpu.SemaphoreType.DMA((7,)),
            pltpu.SemaphoreType.DMA((4,)),
        ],
        compiler_params=pltpu.CompilerParams(vmem_limit_bytes=VMEM_LIMIT),
        cost_estimate=pl.CostEstimate(flops=4_000_000, bytes_accessed=4_000_000, transcendentals=0),
    )(peak, uq, ukv, jnp.transpose(q_weight.reshape(heads, qw)), kv_weight.reshape(heads, kvw), mq, mkv)
    return (
        jnp.transpose(wq).reshape(q_weight.shape),
        wkv.reshape(kv_weight.shape),
        jnp.transpose(mq).reshape(q_moment.shape),
        mkv.reshape(kv_moment.shape),
    )


def solution(mesh):
    in_specs = (
        P(None, "dp", "ctx", None),
        P(None, "dp", "ctx", None),
        P("ctx", None, "dp", None, None),
        P("ctx", None, "dp", None, None),
        P(None, "ctx", "dp", None),
        P(None, "ctx", "dp", None),
        P("dp", "ctx", None),
        P(),
    )
    out_specs = (
        P(None, "dp", "ctx", None),
        P(None, "dp", "ctx", None),
        P(None, "ctx", "dp", None),
        P(None, "ctx", "dp", None),
    )
    return jax.shard_map(local, mesh=mesh, in_specs=in_specs, out_specs=out_specs, check_vma=False)
```

time: 89.3 us -> 81.5 us (0.913)
  local copies, waits for them, and re-layouts: 6.94 us -> 0 us
    unnamed x18 -> x0, local copies, waits for them, and re-layouts: 6.94 us -> none
    pallas_call x1 -> x2, Pallas kernels: 81.1 us -> 80.6 us  [the longest x1 78.2 us: local(): pl.pallas_call(kernel, out_shape=(jax.ShapeDtypeStruct((qw, heads), BF),...]
where the time goes in v1:
time: 81.5 us; the launch traced here: 81.3 us
  Pallas kernels  80.6 us (99%)
    pallas_call x1, Pallas kernels, local(): pl.pallas_call(kernel, out_shape=(jax.ShapeDtypeStruct((qw, heads), BF),...  78.2 us
    pallas_call x1, Pallas kernels, local(): pl.pallas_call(finish, out_shape=(jax.ShapeDtypeStruct((qw, heads), BF),...  2.42 us

profile of v1, /device:TPU:1, one launch (start us, length us, event | category | flops | bytes accessed | tf_op | source)
XLA Modules:
  0.0 81.3 jit_solution(16825783129876931275)
XLA Ops:
  0.6 78.2 %shard_map.111 = (bf16[576,256]{1,0:T(8,128)(2,1)}, bf16[256,256]{1,0:T(8,128)(2,1)}, f32[576,256]{1,0:T(8,128)}, f32[512,128]{1,0:T(8,128)}, f32[1,256]{1,0:T(1,128)}) custom-call(s32[1,256]{1,0:T(1,128)} %bitcast.36, f32[1,256]{1,0:T(1,128)} %bitcast.37, bf16[2,576,256]{2,1,0:T(8,128)(2,1)} %bitcast.28, bf16[1024,128]{1,0:T(8,128)(2,1)} %bitcast.32, ...), custom_call_target="tpu_custom_call" | custom-call | flops 4000000000 | bytes 4000000 | tf_op jit(solution)/shard_map/pallas_call | solution.py:459
  78.9 2.4 %shard_map.112 = (bf16[576,256]{1,0:T(8,128)(2,1)}, bf16[256,256]{1,0:T(8,128)(2,1)}, f32[576,256]{1,0:T(8,128)}, f32[512,128]{1,0:T(8,128)}) custom-call(f32[1,256]{1,0:T(1,128)} %get-tuple-element.13.peak_hbm, bf16[576,256]{1,0:T(8,128)(2,1)} %get-tuple-element.14.uq_hbm, bf16[256,256]{1,0:T(8,128)(2,1)} %get-tuple-element.15.ukv_hbm, ...), custom_call_target="tpu_custom_call" | custom-call | flops 4000000 | bytes 4000000 | tf_op jit(solution)/shard_map/pallas_call | solution.py:522

commit v2 on v1

--- a/solution.py
+++ b/solution.py
@@ -36,6 +36,7 @@
 CHUNKS = (256, 384, 256)
 Q_CUTS = ((0, 256), (256, 640))
 Q_PAD = 640
+Z_FIRST = 1
 VMEM_LIMIT = 62 * 1024 * 1024
 
 
@@ -60,7 +61,7 @@
     uq_hbm, ukv_hbm, mq_new_hbm, mkv_new_hbm, peak_hbm,
     slot_ref, logit_ref, gq_ref, gkv_ref, mq_ref, mkv_ref,
     uq_out, ukv_out, mq_out, mkv_out, peak_out,
-    xq, xkv, okv, skv, qs, place, swap,
+    xq, xkv, okv, skv, qs, place, pick, swap,
     fsa0, fsa1, fsa2, fra0, fra1, fra2, fsb0, fsb1, fsb2, frb0, frb1, frb2,
     bsa0, bsa1, bsa2, bra0, bra1, bra2, bsb0, bsb1, bsb2, brb0, brb1, brb2,
     mbq, mpq, mbkv, mpkv, xt, xk, xf,
@@ -137,20 +138,21 @@
     loads[4].wait()
     rows = lax.broadcasted_iota(jnp.int32, (total, heads), 0)
     place[...] = one_hot(slot_ref[...] == (rows % GYX) * GZ + rows // GYX)
+    pick[...] = one_hot(slot_ref[...] == rows)
     rows = lax.broadcasted_iota(jnp.int32, (total, total), 0)
     cols = lax.broadcasted_iota(jnp.int32, (total, total), 1)
     swap[...] = one_hot(cols == (rows % GZ) * GYX + rows // GZ)
     qs[qw:, :] = jnp.zeros((Q_PAD - qw, heads), BF)
     xf[qw:, :] = jnp.zeros((Q_PAD - qw, total), BF)
 
+    def pick_rows(dst, half):
+        cols = lax.broadcasted_iota(jnp.int32, (heads, 2 * halves * heads), 1)
+        rows = lax.broadcasted_iota(jnp.int32, (heads, 2 * halves * heads), 0)
+        offset = cols - 2 * halves * rows
+        for t in range(halves):
+            dst[:, t * lanes : (t + 1) * lanes] = nn(one_hot(offset == 2 * t + half), gkv_ref[...]).astype(BF)
+
     loads[1].wait()
-    cols = lax.broadcasted_iota(jnp.int32, (heads, 2 * halves * heads), 1)
-    rows = lax.broadcasted_iota(jnp.int32, (heads, 2 * halves * heads), 0)
-    offset = cols - 2 * halves * rows
-    for t in range(halves):
-        band = slice(t * lanes, (t + 1) * lanes)
-        okv[:, band] = nn(one_hot(offset == 2 * t + other), gkv_ref[...]).astype(BF)
-        skv[:, band] = nn(one_hot(offset == 2 * t + core), gkv_ref[...]).astype(BF)
     loads[0].wait()
     loads[5].wait()
 
@@ -165,8 +167,9 @@
     spans = tuple(slice(low, min(high, qw)) for low, high in Q_CUTS)
     core_q = [to_core(gq_ref.at[other, span], xq.at[span], n) for n, span in enumerate(spans)]
     core_kv = to_core(okv, xkv, 2)
-    for copy in core_q:
+    for copy in core_q[::-1]:
         copy.start()
+    pick_rows(okv, other)
     core_kv.start()
 
     def send_z(src, dst, send_sem, recv_sem, zt):
@@ -180,18 +183,6 @@
     def keep_z(src, dst):
         mine = pl.ds(pl.multiple_of(z * GYX, GYX), GYX)
         dst[mine, :] = src[mine, :]
-
-    def some_z(n, parity):
-        odd = lax.rem(z + parity, 2)
-
-        def body(i, carry):
-            j = i + 1 - odd
-            step = GZ // 2 - odd - 2 * (j // 2)
-            sign = 1 - 2 * (j % 2)
-            send_z(fsa[n], fra[n], fa_send.at[n], fa_recv.at[n], lax.rem(z + sign * step + GZ, GZ))
-            return carry
-
-        lax.fori_loop(0, GZ // 2 - 1 + odd, body, 0)
 
     def all_z(src, dst, send_sem, recv_sem):
         def body(i, carry):
@@ -243,32 +234,37 @@
     lax.fori_loop(0, GZ - 1, logits_z, 0)
     lz[z] = logit_ref[...]
 
-    for n, (low, high) in enumerate(Q_CUTS):
+    for n in (1, 0):
         core_q[n].wait()
+        low, high = Q_CUTS[n]
         span = spans[n]
         qs[span, :] = (gq_ref[core, span].astype(F32) + xq[span, :].astype(F32)).astype(BF)
-        fsa[n][...] = nt(place[...], qs[low:high, :]).astype(BF)
-        some_z(n, 0)
-    for n in range(2):
-        some_z(n, 1)
-        keep_z(fsa[n], fra[n])
+        if n == Z_FIRST:
+            fsa[n][...] = nt(place[...], qs[low:high, :]).astype(BF)
+            all_z(fsa[n], fra[n], fa_send.at[n], fa_recv.at[n])
+        else:
+            fsa[n][...] = nt(pick[...], qs[low:high, :]).astype(BF)
+            all_yx(fsa[n], fra[n], fa_send.at[n], fa_recv.at[n])
+    pick_rows(skv, core)
     core_kv.wait()
     kvs = (skv[...].astype(F32) + xkv[...].astype(F32)).astype(BF)
-    fsa[2][...] = nn(place[...], kvs).astype(BF)
-    some_z(2, 0)
-    some_z(2, 1)
-    keep_z(fsa[2], fra[2])
+    fsa[2][...] = nn(pick[...], kvs).astype(BF)
+    all_yx(fsa[2], fra[2], fa_send.at[2], fa_recv.at[2])
+
+    def second_leg(n, src, mid, dst, first_recv, send_sem, recv_sem):
+        wait_rows(src, (GZ - 1) * GYX, first_recv)
+        mid[...] = nn(swap[...], src[...]).astype(BF)
+        leg = all_yx if n == Z_FIRST else all_z
+        leg(mid, dst, send_sem, recv_sem)
 
     def forward_mid(n):
-        wait_z(fra[n], fa_recv.at[n])
-        fsb[n][...] = nn(swap[...], fra[n][...]).astype(BF)
-        all_yx(fsb[n], frb[n], fb_send.at[n], fb_recv.at[n])
+        second_leg(n, fra[n], fsb[n], frb[n], fa_recv.at[n], fb_send.at[n], fb_recv.at[n])
 
     loads[2].wait()
     loads[3].wait()
     forward_mid(0)
+    forward_mid(2)
     forward_mid(1)
-    forward_mid(2)
 
     view = lz.at[pl.ds(0, GZ - 1)]
     pltpu.make_async_copy(view, view, log_recv.at[0]).wait()
@@ -283,10 +279,14 @@
         span = spans[n]
         real = min(high, qw) - low
         size = high - low
-        eye = one_hot(
-            lax.broadcasted_iota(jnp.int32, (real, size), 0) == lax.broadcasted_iota(jnp.int32, (real, size), 1)
-        )
-        fresh = momentum_rate * mq_ref[span, :] + nt(eye, frb[n][...])
+        if n == Z_FIRST:
+            eye = one_hot(
+                lax.broadcasted_iota(jnp.int32, (real, size), 0) == lax.broadcasted_iota(jnp.int32, (real, size), 1)
+            )
+            arrived = nt(eye, frb[n][...])
+        else:
+            arrived = tn(frb[n][...], swap[...])[:real, :]
+        fresh = momentum_rate * mq_ref[span, :] + arrived
         mq_out[span, :] = fresh
         mbq[span, :] = fresh.astype(BF)
         core_mq[n].start()
@@ -318,15 +318,24 @@
         j = low // total
         xf[j * QDIM : (j + 1) * QDIM, :] = piece
 
-    for n, (low, high) in enumerate(Q_CUTS):
-        bsa[n][...] = nt(swap[...], xf[low:high, :]).astype(BF)
-        all_z(bsa[n], bra[n], ba_send.at[n], ba_recv.at[n])
+    same = one_hot(
+        lax.broadcasted_iota(jnp.int32, (total, total), 0) == lax.broadcasted_iota(jnp.int32, (total, total), 1)
+    )
+    for n in (1, 0):
+        low, high = Q_CUTS[n]
+        if n == Z_FIRST:
+            bsa[n][...] = nt(swap[...], xf[low:high, :]).astype(BF)
+            all_z(bsa[n], bra[n], ba_send.at[n], ba_recv.at[n])
+        else:
+            bsa[n][...] = nt(same, xf[low:high, :]).astype(BF)
+            all_yx(bsa[n], bra[n], ba_send.at[n], ba_recv.at[n])
 
     wait_yx(frb[2], fb_recv.at[2])
+    arrived = nn(swap[...], frb[2][...])
     for t in range(halves):
         band = slice(t * lanes, (t + 1) * lanes)
         picked = pl.ds(t, total, stride=halves)
-        fresh = momentum_rate * mkv_ref[picked, :] + frb[2][:, band].astype(F32)
+        fresh = momentum_rate * mkv_ref[picked, :] + arrived[:, band]
         mkv_out[picked, :] = fresh
         mbkv[:, band] = fresh.astype(BF)
     core_mkv = to_core(mbkv, mpkv, 5)
@@ -350,8 +359,13 @@
         for low, piece in newton(xk, 2 * total):
             xk[:, low : low + total] = piece
     for low, piece in newton(xk, total):
-        bsa[2][...] = nt(swap[...], piece).astype(BF)
-    all_z(bsa[2], bra[2], ba_send.at[2], ba_recv.at[2])
+        bsa[2][...] = nt(same, piece).astype(BF)
+    all_yx(bsa[2], bra[2], ba_send.at[2], ba_recv.at[2])
+
+    def back_mid(n):
+        second_leg(n, bra[n], bsb[n], brb[n], ba_recv.at[n], bb_send.at[n], bb_recv.at[n])
+
+    back_mid(0)
 
     view = ly.at[pl.ds(0, GYX - 1)]
     pltpu.make_async_copy(view, view, log_recv.at[1]).wait()
@@ -362,20 +376,14 @@
     peak_out[...] = jnp.maximum(lc[...], lp[...])
     stores[4].start()
 
-    def back_mid(n):
-        wait_z(bra[n], ba_recv.at[n])
-        bsb[n][...] = nn(swap[...], bra[n][...]).astype(BF)
-        all_yx(bsb[n], brb[n], bb_send.at[n], bb_recv.at[n])
-
-    back_mid(0)
+    back_mid(2)
     back_mid(1)
-    back_mid(2)
-
-    pick = one_hot(slot_ref[...] == lax.broadcasted_iota(jnp.int32, (total, heads), 0))
+
     for n, (low, high) in enumerate(Q_CUTS):
         wait_yx(brb[n], bb_recv.at[n])
         real = min(high, qw) - low
-        uq_out[spans[n], :] = tn(brb[n][...], pick)[:real, :].astype(BF)
+        order = pick if n == Z_FIRST else place
+        uq_out[spans[n], :] = tn(brb[n][...], order[...])[:real, :].astype(BF)
     stores[0].start()
     for n in range(3):
         wait_z(fsa[n], fa_send.at[n])
@@ -386,7 +394,7 @@
     view = ly.at[pl.ds(0, GYX - 1)]
     pltpu.make_async_copy(view, view, log_send.at[1]).wait()
     wait_yx(brb[2], bb_recv.at[2])
-    ukv_out[...] = tn(pick, brb[2][...]).astype(BF)
+    ukv_out[...] = tn(place[...], brb[2][...]).astype(BF)
     stores[1].start()
     for n in range(3):
         wait_yx(bsb[n], bb_send.at[n])
@@ -484,6 +492,7 @@
             pltpu.VMEM((heads, kvw), BF),
             pltpu.VMEM((heads, kvw), BF),
             pltpu.VMEM((Q_PAD, heads), BF),
+            pltpu.VMEM((total, heads), BF),
             pltpu.VMEM((total, heads), BF),
             pltpu.VMEM((total, total), BF),
             *travel,

time: 81.5 us -> 69.8 us (0.86)
  Pallas kernels: 80.6 us -> 69 us
    pallas_call x1, Pallas kernels: 78.2 us -> 66.5 us  [local(): pl.pallas_call(kernel, out_shape=(jax.ShapeDtypeStruct((qw, heads), BF),...]
where the time goes in v2:
time: 69.8 us; the launch traced here: 69.6 us
  Pallas kernels  69 us (99%)
    pallas_call x1, Pallas kernels, local(): pl.pallas_call(kernel, out_shape=(jax.ShapeDtypeStruct((qw, heads), BF),...  66.5 us
    pallas_call x1, Pallas kernels, local(): pl.pallas_call(finish, out_shape=(jax.ShapeDtypeStruct((qw, heads), BF),...  2.42 us

profile of v2, /device:TPU:1, one launch (start us, length us, event | category | flops | bytes accessed | tf_op | source)
XLA Modules:
  0.0 69.6 jit_solution(1635212665378200485)
XLA Ops:
  0.6 66.5 %shard_map.111 = (bf16[576,256]{1,0:T(8,128)(2,1)}, bf16[256,256]{1,0:T(8,128)(2,1)}, f32[576,256]{1,0:T(8,128)}, f32[512,128]{1,0:T(8,128)}, f32[1,256]{1,0:T(1,128)}) custom-call(s32[1,256]{1,0:T(1,128)} %bitcast.36, f32[1,256]{1,0:T(1,128)} %bitcast.37, bf16[2,576,256]{2,1,0:T(8,128)(2,1)} %bitcast.28, bf16[1024,128]{1,0:T(8,128)(2,1)} %bitcast.32, ...), custom_call_target="tpu_custom_call" | custom-call | flops 4000000000 | bytes 4000000 | tf_op jit(solution)/shard_map/pallas_call | solution.py:467
  67.2 2.4 %shard_map.112 = (bf16[576,256]{1,0:T(8,128)(2,1)}, bf16[256,256]{1,0:T(8,128)(2,1)}, f32[576,256]{1,0:T(8,128)}, f32[512,128]{1,0:T(8,128)}) custom-call(f32[1,256]{1,0:T(1,128)} %get-tuple-element.13.peak_hbm, bf16[576,256]{1,0:T(8,128)(2,1)} %get-tuple-element.14.uq_hbm, bf16[256,256]{1,0:T(8,128)(2,1)} %get-tuple-element.15.ukv_hbm, ...), custom_call_target="tpu_custom_call" | custom-call | flops 4000000 | bytes 4000000 | tf_op jit(solution)/shard_map/pallas_call | solution.py:531

commit v3 on v2

--- a/solution.py
+++ b/solution.py
@@ -272,9 +272,9 @@
     lax.fori_loop(0, GYX - 1, logits_yx, 0)
     ly[yx] = lm[...]
 
-    squares = jnp.zeros((1, 1), F32)
     core_mq = [to_core(mbq.at[span], mpq.at[span], 3 + n) for n, span in enumerate(spans)]
-    for n, (low, high) in enumerate(Q_CUTS):
+    for n in (1, 0):
+        low, high = Q_CUTS[n]
         wait_yx(frb[n], fb_recv.at[n])
         span = spans[n]
         real = min(high, qw) - low
@@ -287,31 +287,38 @@
         else:
             arrived = tn(frb[n][...], swap[...])[:real, :]
         fresh = momentum_rate * mq_ref[span, :] + arrived
-        mq_out[span, :] = fresh
         mbq[span, :] = fresh.astype(BF)
         core_mq[n].start()
-        squares = squares + jnp.sum(fresh * fresh, keepdims=True)
-    for n, span in enumerate(spans):
-        core_mq[n].wait()
-        theirs = mpq[span, :].astype(F32)
-        squares = squares + jnp.sum(theirs * theirs, keepdims=True)
+        mq_out[span, :] = fresh
     stores[2].start()
-    scale = 1.0 / (jnp.sqrt(squares) + norm_eps)
-    parts = qw // QDIM
-    for j in range(parts):
-        band = slice(j * QDIM, (j + 1) * QDIM)
-        xt[:, j * total : (j + 1) * total] = (mq_out[band, :] * scale).astype(BF)
-        lane = (parts + j) * total
-        xt[:, lane : lane + total] = (mpq[band, :].astype(F32) * scale).astype(BF)
+
+    def grams(ref):
+        return sum(nt(ref[j * QDIM : (j + 1) * QDIM, :], ref[j * QDIM : (j + 1) * QDIM, :]) for j in range(parts))
+
+    def mix(gram):
+        return (newton_b * gram.astype(F32) + newton_c * nn(gram, gram)).astype(BF)
 
     def newton(ref, width):
-        gram = nt(ref[...], ref[...]).astype(BF)
-        mixer = (newton_b * gram.astype(F32) + newton_c * nn(gram, gram)).astype(BF)
+        mixer = mix(nt(ref[...], ref[...]).astype(BF))
         for low in range(0, width, total):
             piece = ref[:, low : low + total]
             yield low, (newton_a * piece.astype(F32) + nn(mixer, piece)).astype(BF)
 
-    for iteration in range(ITERS - 1):
+    parts = qw // QDIM
+    raw = grams(mbq)
+    for n in (1, 0):
+        core_mq[n].wait()
+    raw = raw + grams(mpq)
+    diagonal = lax.broadcasted_iota(jnp.int32, raw.shape, 0) == lax.broadcasted_iota(jnp.int32, raw.shape, 1)
+    squares = jnp.sum(jnp.where(diagonal, raw, 0.0), keepdims=True)
+    scale = 1.0 / (jnp.sqrt(squares) + norm_eps)
+    mixer = mix((raw * scale * scale).astype(BF))
+    for j in range(parts):
+        band = slice(j * QDIM, (j + 1) * QDIM)
+        for lane, ref in ((j * total, mq_out), ((parts + j) * total, mpq)):
+            piece = (ref[band, :].astype(F32) * scale).astype(BF)
+            xt[:, lane : lane + total] = (newton_a * piece.astype(F32) + nn(mixer, piece)).astype(BF)
+    for iteration in range(1, ITERS - 1):
         for low, piece in newton(xt, 2 * parts * total):
             xt[:, low : low + total] = piece
     for low, piece in newton(xt, parts * total):
@@ -329,6 +336,9 @@
         else:
             bsa[n][...] = nt(same, xf[low:high, :]).astype(BF)
             all_yx(bsa[n], bra[n], ba_send.at[n], ba_recv.at[n])
+
+    def back_mid(n):
+        second_leg(n, bra[n], bsb[n], brb[n], ba_recv.at[n], bb_send.at[n], bb_recv.at[n])
 
     wait_yx(frb[2], fb_recv.at[2])
     arrived = nn(swap[...], frb[2][...])
@@ -356,16 +366,13 @@
         xk[band, :total] = nt(eye, (ours * scale).astype(BF)).astype(BF)
         xk[band, total:] = nt(eye, (theirs[:, band] * scale).astype(BF)).astype(BF)
     for iteration in range(ITERS - 1):
+        if iteration == 2:
+            back_mid(0)
         for low, piece in newton(xk, 2 * total):
             xk[:, low : low + total] = piece
     for low, piece in newton(xk, total):
         bsa[2][...] = nt(same, piece).astype(BF)
     all_yx(bsa[2], bra[2], ba_send.at[2], ba_recv.at[2])
-
-    def back_mid(n):
-        second_leg(n, bra[n], bsb[n], brb[n], ba_recv.at[n], bb_send.at[n], bb_recv.at[n])
-
-    back_mid(0)
 
     view = ly.at[pl.ds(0, GYX - 1)]
     pltpu.make_async_copy(view, view, log_recv.at[1]).wait()

time: 69.8 us -> 69.8 us (level)
  no operation moved by 1% of the time
where the time goes in v3:
time: 69.8 us; the launch traced here: 69.6 us
  Pallas kernels  69 us (99%)
    pallas_call x1, Pallas kernels, local(): pl.pallas_call(kernel, out_shape=(jax.ShapeDtypeStruct((qw, heads), BF),...  66.6 us
    pallas_call x1, Pallas kernels, local(): pl.pallas_call(finish, out_shape=(jax.ShapeDtypeStruct((qw, heads), BF),...  2.42 us

profile of v3, /device:TPU:1, one launch (start us, length us, event | category | flops | bytes accessed | tf_op | source)
XLA Modules:
  0.0 69.6 jit_solution(14188789633255721988)
XLA Ops:
  0.6 66.6 %shard_map.111 = (bf16[576,256]{1,0:T(8,128)(2,1)}, bf16[256,256]{1,0:T(8,128)(2,1)}, f32[576,256]{1,0:T(8,128)}, f32[512,128]{1,0:T(8,128)}, f32[1,256]{1,0:T(1,128)}) custom-call(s32[1,256]{1,0:T(1,128)} %bitcast.36, f32[1,256]{1,0:T(1,128)} %bitcast.37, bf16[2,576,256]{2,1,0:T(8,128)(2,1)} %bitcast.28, bf16[1024,128]{1,0:T(8,128)(2,1)} %bitcast.32, ...), custom_call_target="tpu_custom_call" | custom-call | flops 4000000000 | bytes 4000000 | tf_op jit(solution)/shard_map/pallas_call | solution.py:474
  67.2 2.4 %shard_map.112 = (bf16[576,256]{1,0:T(8,128)(2,1)}, bf16[256,256]{1,0:T(8,128)(2,1)}, f32[576,256]{1,0:T(8,128)}, f32[512,128]{1,0:T(8,128)}) custom-call(f32[1,256]{1,0:T(1,128)} %get-tuple-element.13.peak_hbm, bf16[576,256]{1,0:T(8,128)(2,1)} %get-tuple-element.14.uq_hbm, bf16[256,256]{1,0:T(8,128)(2,1)} %get-tuple-element.15.ukv_hbm, ...), custom_call_target="tpu_custom_call" | custom-call | flops 4000000 | bytes 4000000 | tf_op jit(solution)/shard_map/pallas_call | solution.py:538

commit v4 on v2

--- a/solution.py
+++ b/solution.py
@@ -416,7 +416,7 @@
             )
         )
     ]
-    for load in loads:
+    for load in loads[5:] + loads[:5]:
         load.start()
     copies = [
         pltpu.make_async_copy(src, dst, sem.at[n])
@@ -425,6 +425,9 @@
         )
     ]
     qw, heads = wq_ref.shape
+    for n in (5, 6):
+        loads[n].wait()
+        copies[n - 5].start()
     for load in loads[:3]:
         load.wait()
     clip = jnp.minimum(1.0, clip_limit / peak_ref[...])
@@ -436,10 +439,6 @@
             fresh = wide - learn_rate * (scale * uq_ref[start:stop, :].astype(F32) + weight_decay * wide)
             new_q[start:stop, :] = (fresh * factor).astype(BF)
     copies[2].start()
-    for load in loads[5:]:
-        load.wait()
-    copies[0].start()
-    copies[1].start()
     for load in loads[3:5]:
         load.wait()
     scale = rms_match * math.sqrt(max(KVRANK, KVDIM))

time: 69.8 us -> 69.7 us (level)
  no operation moved by 1% of the time
where the time goes in v4:
time: 69.7 us; the launch traced here: 69.5 us
  Pallas kernels  68.9 us (99%)
    pallas_call x1, Pallas kernels, local(): pl.pallas_call(kernel, out_shape=(jax.ShapeDtypeStruct((qw, heads), BF),...  66.5 us
    pallas_call x1, Pallas kernels, local(): pl.pallas_call(finish, out_shape=(jax.ShapeDtypeStruct((qw, heads), BF),...  2.34 us

profile of v4, /device:TPU:1, one launch (start us, length us, event | category | flops | bytes accessed | tf_op | source)
XLA Modules:
  0.0 69.5 jit_solution(14025572795036492495)
XLA Ops:
  0.6 66.5 %shard_map.111 = (bf16[576,256]{1,0:T(8,128)(2,1)}, bf16[256,256]{1,0:T(8,128)(2,1)}, f32[576,256]{1,0:T(8,128)}, f32[512,128]{1,0:T(8,128)}, f32[1,256]{1,0:T(1,128)}) custom-call(s32[1,256]{1,0:T(1,128)} %bitcast.36, f32[1,256]{1,0:T(1,128)} %bitcast.37, bf16[2,576,256]{2,1,0:T(8,128)(2,1)} %bitcast.28, bf16[1024,128]{1,0:T(8,128)(2,1)} %bitcast.32, ...), custom_call_target="tpu_custom_call" | custom-call | flops 4000000000 | bytes 4000000 | tf_op jit(solution)/shard_map/pallas_call | solution.py:466
  67.2 2.3 %shard_map.112 = (bf16[576,256]{1,0:T(8,128)(2,1)}, bf16[256,256]{1,0:T(8,128)(2,1)}, f32[576,256]{1,0:T(8,128)}, f32[512,128]{1,0:T(8,128)}) custom-call(f32[1,256]{1,0:T(1,128)} %get-tuple-element.13.peak_hbm, bf16[576,256]{1,0:T(8,128)(2,1)} %get-tuple-element.14.uq_hbm, bf16[256,256]{1,0:T(8,128)(2,1)} %get-tuple-element.15.ukv_hbm, ...), custom_call_target="tpu_custom_call" | custom-call | flops 4000000 | bytes 4000000 | tf_op jit(solution)/shard_map/pallas_call | solution.py:530
